TPU v7x, 128 devices: a whole 4x4x4 slice. The times are simulated.
128 devices in a mesh: pipe: 8 (over z, core), tensor: 16 (over x, y).
Axes of the slice: x: 4, y: 4, z: 4, core: 2. Of those that a mesh axis runs over, the one named last changes fastest.
Arguments:
- tokens: bfloat16 [8, 128, 4096], P(None, 'tensor'), may hold values from -60 to 60
- norm_gain: float32 [8, 4096], P('pipe'), may hold values from 0.25 to 1.75
- gate_weight: bfloat16 [8, 4096, 14336], P('pipe', None, 'tensor'), may hold values from -0.09375 to 0.09375
- up_weight: bfloat16 [8, 4096, 14336], P('pipe', None, 'tensor'), may hold values from -0.09375 to 0.09375
- down_weight: bfloat16 [8, 14336, 4096], P('pipe', 'tensor'), may hold values from -0.046875 to 0.046875
Outputs:
- states: bfloat16 [8, 8, 128, 4096], P('pipe', None, 'tensor')
All inputs are finite; a program needn't handle non-finite values.
Results may differ from a plain program's by a relative error of at most 0.019.
Values may be sent and summed in bfloat16 or wider, within the bound.
A program may use at most 128 MiB of HBM per device.

v0:
```python
import jax
import jax.numpy as jnp
from jax import lax
from jax.sharding import PartitionSpec as P


def passed_along(value, axis, steps):
    count = lax.axis_size(axis)
    leading, last = (max(0, -steps), min(count, count - steps))
    return lax.ppermute(value, axis, [(source, source + steps) for source in range(leading, last)])


def normalize(row_block, scale_gain):
    values = row_block.astype(jnp.float32)
    inv_rms = lax.rsqrt(jnp.mean(values * values, axis=-1, keepdims=True) + 1e-05)
    return (values * inv_rms * scale_gain).astype(jnp.bfloat16)


def swiglu(normed, w_gate, w_up):
    gate_out = jnp.dot(normed, w_gate, preferred_element_type=jnp.float32)
    up_out = jnp.dot(normed, w_up, preferred_element_type=jnp.float32)
    return (jax.nn.silu(gate_out) * up_out).astype(jnp.bfloat16)


def apply_layer(current, scale_gain, w_gate, w_up, w_down):
    normed = normalize(current, scale_gain)
    hidden = swiglu(lax.all_gather(normed, "tensor", axis=0, tiled=True), w_gate, w_up)
    branch = lax.psum_scatter(
        jnp.dot(hidden, w_down, preferred_element_type=jnp.float32),
        "tensor",
        scatter_dimension=0,
        tiled=True,
    )
    return (current.astype(jnp.float32) + branch).astype(jnp.bfloat16)


def hand_over(row_block):
    return passed_along(row_block, "pipe", 1)


def local(tokens, norm_gain, gate_weight, up_weight, down_weight):
    batches, own_rows, feature_dim = tokens.shape
    section_layers = gate_weight.shape[0]
    pieces = 1
    blocks = batches * pieces
    block_rows = own_rows // pieces
    sections = lax.axis_size("pipe")
    section_idx = lax.axis_index("pipe")

    def advance(loop_state, tick_idx):
        incoming, states = loop_state
        block_idx = tick_idx - section_idx
        is_live = (block_idx >= 0) & (block_idx < blocks)
        store_at = jnp.clip(block_idx, 0, blocks - 1)
        enter_at = jnp.clip(tick_idx, 0, blocks - 1)
        entering = lax.dynamic_index_in_dim(tokens, enter_at, 0, keepdims=False)
        current = jnp.where(section_idx == 0, entering, incoming)
        current = apply_layer(current, norm_gain[0], gate_weight[0], up_weight[0], down_weight[0])
        outputs = [current]
        stacked = jnp.stack(outputs)[:, None]
        previous = lax.dynamic_slice_in_dim(states, store_at, 1, 1)
        states = lax.dynamic_update_slice_in_dim(
            states, jnp.where(is_live, stacked, previous), store_at, 1
        )
        return ((hand_over(current), states), None)

    start_states = jnp.zeros((section_layers, blocks, block_rows, feature_dim), jnp.bfloat16)
    start_rows = jnp.zeros((block_rows, feature_dim), jnp.bfloat16)
    ticks_all = jnp.arange(blocks + sections - 1, dtype=jnp.int32)
    (last_rows, states), _ = lax.scan(advance, (start_rows, start_states), ticks_all)
    return states


def solution(mesh):
    in_specs = (
        P(None, "tensor", None),
        P("pipe", None),
        P("pipe", None, "tensor"),
        P("pipe", None, "tensor"),
        P("pipe", "tensor", None),
    )
    out_specs = P("pipe", None, "tensor", None)
    return jax.shard_map(local, mesh=mesh, in_specs=in_specs, out_specs=out_specs, check_vma=False)
```

profile of v0, /device:TPU:97, one launch (start us, length us, event | category | flops | bytes accessed | tf_op | source)
XLA Modules:
  0.0 2345.8 jit_solution(11557643858708339272)
XLA Ops:
  6.6 2331.6 %while.13 = (s32[]{:T(128)}, bf16[8,4096]{1,0:T(8,128)(2,1)S(1)}, bf16[1,8,8,4096]{3,2,1,0:T(8,128)(2,1)S(1)}, pred[]{:T(512)}, s32[15]{0:T(128)S(1)}, /*index=5...) while((s32[]{:T(128)}, bf16[8,4096]{1,0:T(8,128)(2,1)S(1)}, ...), condition=%wide.region_3.4_spmd, body=%wide.region_0.3_spmd.sunk | while | flops 2820177920 | bytes 48253548 | solution.py:70
  10.3 42.5 %all-gather.2.cloned.1.call-done = bf16[128,4096]{1,0:T(8,128)(2,1)} async-done(((bf16[8,4096]{1,0:T(8,128)(2,1)}), bf16[128,4096]{1,0:T(8,128)(2,1)}) %all-gather.2.cloned.1.call-update) | async-done | bytes 1048592 | tf_op jit(solution)/shard_map/while/body/eval_jaxpr/all_gather | solution.py:27
  52.9 4.8 fusion.46
  57.7 8.9 fusion.47
  68.4 88.0 %all-reduce.5.cloned.1.call-done = f32[128,4096]{1,0:T(8,128)} async-done(((f32[128,4096]{1,0:T(8,128)}), f32[128,4096]{1,0:T(8,128)}) %all-reduce.5.cloned.1.call-update) | async-done | bytes 2097168 | tf_op jit(solution)/shard_map/while
  158.6 3.1 collective-permute-done
  165.4 42.9 %all-gather.2.cloned.1.call-done = bf16[128,4096]{1,0:T(8,128)(2,1)} async-done(((bf16[8,4096]{1,0:T(8,128)(2,1)}), bf16[128,4096]{1,0:T(8,128)(2,1)}) %all-gather.2.cloned.1.call-update) | async-done | bytes 1048592 | tf_op jit(solution)/shard_map/while/body/eval_jaxpr/all_gather | solution.py:27
  208.3 4.8 fusion.46
  213.1 8.9 fusion.47
  223.8 88.0 %all-reduce.5.cloned.1.call-done = f32[128,4096]{1,0:T(8,128)} async-done(((f32[128,4096]{1,0:T(8,128)}), f32[128,4096]{1,0:T(8,128)}) %all-reduce.5.cloned.1.call-update) | async-done | bytes 2097168 | tf_op jit(solution)/shard_map/while
  314.1 3.1 collective-permute-done
  320.9 42.9 %all-gather.2.cloned.1.call-done = bf16[128,4096]{1,0:T(8,128)(2,1)} async-done(((bf16[8,4096]{1,0:T(8,128)(2,1)}), bf16[128,4096]{1,0:T(8,128)(2,1)}) %all-gather.2.cloned.1.call-update) | async-done | bytes 1048592 | tf_op jit(solution)/shard_map/while/body/eval_jaxpr/all_gather | solution.py:27
  363.8 4.8 fusion.46
  368.6 8.9 fusion.47
  379.3 88.0 %all-reduce.5.cloned.1.call-done = f32[128,4096]{1,0:T(8,128)} async-done(((f32[128,4096]{1,0:T(8,128)}), f32[128,4096]{1,0:T(8,128)}) %all-reduce.5.cloned.1.call-update) | async-done | bytes 2097168 | tf_op jit(solution)/shard_map/while
  469.6 3.1 collective-permute-done
  476.3 42.9 %all-gather.2.cloned.1.call-done = bf16[128,4096]{1,0:T(8,128)(2,1)} async-done(((bf16[8,4096]{1,0:T(8,128)(2,1)}), bf16[128,4096]{1,0:T(8,128)(2,1)}) %all-gather.2.cloned.1.call-update) | async-done | bytes 1048592 | tf_op jit(solution)/shard_map/while/body/eval_jaxpr/all_gather | solution.py:27
  519.3 4.8 fusion.46
  524.1 8.9 fusion.47
  534.8 88.0 %all-reduce.5.cloned.1.call-done = f32[128,4096]{1,0:T(8,128)} async-done(((f32[128,4096]{1,0:T(8,128)}), f32[128,4096]{1,0:T(8,128)}) %all-reduce.5.cloned.1.call-update) | async-done | bytes 2097168 | tf_op jit(solution)/shard_map/while
  631.8 42.9 %all-gather.2.cloned.1.call-done = bf16[128,4096]{1,0:T(8,128)(2,1)} async-done(((bf16[8,4096]{1,0:T(8,128)(2,1)}), bf16[128,4096]{1,0:T(8,128)(2,1)}) %all-gather.2.cloned.1.call-update) | async-done | bytes 1048592 | tf_op jit(solution)/shard_map/while/body/eval_jaxpr/all_gather | solution.py:27
  674.8 4.8 fusion.46
  679.6 8.9 fusion.47
  690.3 88.0 %all-reduce.5.cloned.1.call-done = f32[128,4096]{1,0:T(8,128)} async-done(((f32[128,4096]{1,0:T(8,128)}), f32[128,4096]{1,0:T(8,128)}) %all-reduce.5.cloned.1.call-update) | async-done | bytes 2097168 | tf_op jit(solution)/shard_map/while
  787.3 42.9 %all-gather.2.cloned.1.call-done = bf16[128,4096]{1,0:T(8,128)(2,1)} async-done(((bf16[8,4096]{1,0:T(8,128)(2,1)}), bf16[128,4096]{1,0:T(8,128)(2,1)}) %all-gather.2.cloned.1.call-update) | async-done | bytes 1048592 | tf_op jit(solution)/shard_map/while/body/eval_jaxpr/all_gather | solution.py:27
  830.2 4.8 fusion.46
  835.0 8.9 fusion.47
  845.8 88.0 %all-reduce.5.cloned.1.call-done = f32[128,4096]{1,0:T(8,128)} async-done(((f32[128,4096]{1,0:T(8,128)}), f32[128,4096]{1,0:T(8,128)}) %all-reduce.5.cloned.1.call-update) | async-done | bytes 2097168 | tf_op jit(solution)/shard_map/while
  942.8 42.9 %all-gather.2.cloned.1.call-done = bf16[128,4096]{1,0:T(8,128)(2,1)} async-done(((bf16[8,4096]{1,0:T(8,128)(2,1)}), bf16[128,4096]{1,0:T(8,128)(2,1)}) %all-gather.2.cloned.1.call-update) | async-done | bytes 1048592 | tf_op jit(solution)/shard_map/while/body/eval_jaxpr/all_gather | solution.py:27
  985.7 4.8 fusion.46
  990.5 8.9 fusion.47
  1001.2 88.0 %all-reduce.5.cloned.1.call-done = f32[128,4096]{1,0:T(8,128)} async-done(((f32[128,4096]{1,0:T(8,128)}), f32[128,4096]{1,0:T(8,128)}) %all-reduce.5.cloned.1.call-update) | async-done | bytes 2097168 | tf_op jit(solution)/shard_map/while
  1098.2 42.9 %all-gather.2.cloned.1.call-done = bf16[128,4096]{1,0:T(8,128)(2,1)} async-done(((bf16[8,4096]{1,0:T(8,128)(2,1)}), bf16[128,4096]{1,0:T(8,128)(2,1)}) %all-gather.2.cloned.1.call-update) | async-done | bytes 1048592 | tf_op jit(solution)/shard_map/while/body/eval_jaxpr/all_gather | solution.py:27
  1141.1 4.8 fusion.46
  1145.9 8.9 fusion.47
  1156.7 88.0 %all-reduce.5.cloned.1.call-done = f32[128,4096]{1,0:T(8,128)} async-done(((f32[128,4096]{1,0:T(8,128)}), f32[128,4096]{1,0:T(8,128)}) %all-reduce.5.cloned.1.call-update) | async-done | bytes 2097168 | tf_op jit(solution)/shard_map/while
  1253.7 42.9 %all-gather.2.cloned.1.call-done = bf16[128,4096]{1,0:T(8,128)(2,1)} async-done(((bf16[8,4096]{1,0:T(8,128)(2,1)}), bf16[128,4096]{1,0:T(8,128)(2,1)}) %all-gather.2.cloned.1.call-update) | async-done | bytes 1048592 | tf_op jit(solution)/shard_map/while/body/eval_jaxpr/all_gather | solution.py:27
  1296.6 4.8 fusion.46
  1301.4 8.9 fusion.47
  1312.1 88.0 %all-reduce.5.cloned.1.call-done = f32[128,4096]{1,0:T(8,128)} async-done(((f32[128,4096]{1,0:T(8,128)}), f32[128,4096]{1,0:T(8,128)}) %all-reduce.5.cloned.1.call-update) | async-done | bytes 2097168 | tf_op jit(solution)/shard_map/while
  1409.1 42.9 %all-gather.2.cloned.1.call-done = bf16[128,4096]{1,0:T(8,128)(2,1)} async-done(((bf16[8,4096]{1,0:T(8,128)(2,1)}), bf16[128,4096]{1,0:T(8,128)(2,1)}) %all-gather.2.cloned.1.call-update) | async-done | bytes 1048592 | tf_op jit(solution)/shard_map/while/body/eval_jaxpr/all_gather | solution.py:27
  1452.0 4.8 fusion.46
  1456.8 8.9 fusion.47
  1467.6 88.0 %all-reduce.5.cloned.1.call-done = f32[128,4096]{1,0:T(8,128)} async-done(((f32[128,4096]{1,0:T(8,128)}), f32[128,4096]{1,0:T(8,128)}) %all-reduce.5.cloned.1.call-update) | async-done | bytes 2097168 | tf_op jit(solution)/shard_map/while
  1564.6 42.9 %all-gather.2.cloned.1.call-done = bf16[128,4096]{1,0:T(8,128)(2,1)} async-done(((bf16[8,4096]{1,0:T(8,128)(2,1)}), bf16[128,4096]{1,0:T(8,128)(2,1)}) %all-gather.2.cloned.1.call-update) | async-done | bytes 1048592 | tf_op jit(solution)/shard_map/while/body/eval_jaxpr/all_gather | solution.py:27
  1607.5 4.8 fusion.46
  1612.3 8.9 fusion.47
  1623.0 88.0 %all-reduce.5.cloned.1.call-done = f32[128,4096]{1,0:T(8,128)} async-done(((f32[128,4096]{1,0:T(8,128)}), f32[128,4096]{1,0:T(8,128)}) %all-reduce.5.cloned.1.call-update) | async-done | bytes 2097168 | tf_op jit(solution)/shard_map/while
  1720.0 42.9 %all-gather.2.cloned.1.call-done = bf16[128,4096]{1,0:T(8,128)(2,1)} async-done(((bf16[8,4096]{1,0:T(8,128)(2,1)}), bf16[128,4096]{1,0:T(8,128)(2,1)}) %all-gather.2.cloned.1.call-update) | async-done | bytes 1048592 | tf_op jit(solution)/shard_map/while/body/eval_jaxpr/all_gather | solution.py:27
  1762.9 4.8 fusion.46
  1767.7 8.9 fusion.47
  1778.5 88.0 %all-reduce.5.cloned.1.call-done = f32[128,4096]{1,0:T(8,128)} async-done(((f32[128,4096]{1,0:T(8,128)}), f32[128,4096]{1,0:T(8,128)}) %all-reduce.5.cloned.1.call-update) | async-done | bytes 2097168 | tf_op jit(solution)/shard_map/while
  1875.5 42.9 %all-gather.2.cloned.1.call-done = bf16[128,4096]{1,0:T(8,128)(2,1)} async-done(((bf16[8,4096]{1,0:T(8,128)(2,1)}), bf16[128,4096]{1,0:T(8,128)(2,1)}) %all-gather.2.cloned.1.call-update) | async-done | bytes 1048592 | tf_op jit(solution)/shard_map/while/body/eval_jaxpr/all_gather | solution.py:27
  1918.4 4.8 fusion.46
  1923.2 8.9 fusion.47
  1933.9 88.0 %all-reduce.5.cloned.1.call-done = f32[128,4096]{1,0:T(8,128)} async-done(((f32[128,4096]{1,0:T(8,128)}), f32[128,4096]{1,0:T(8,128)}) %all-reduce.5.cloned.1.call-update) | async-done | bytes 2097168 | tf_op jit(solution)/shard_map/while
  2030.9 42.9 %all-gather.2.cloned.1.call-done = bf16[128,4096]{1,0:T(8,128)(2,1)} async-done(((bf16[8,4096]{1,0:T(8,128)(2,1)}), bf16[128,4096]{1,0:T(8,128)(2,1)}) %all-gather.2.cloned.1.call-update) | async-done | bytes 1048592 | tf_op jit(solution)/shard_map/while/body/eval_jaxpr/all_gather | solution.py:27
  2073.8 4.8 fusion.46
  2078.6 8.9 fusion.47
  2089.4 88.0 %all-reduce.5.cloned.1.call-done = f32[128,4096]{1,0:T(8,128)} async-done(((f32[128,4096]{1,0:T(8,128)}), f32[128,4096]{1,0:T(8,128)}) %all-reduce.5.cloned.1.call-update) | async-done | bytes 2097168 | tf_op jit(solution)/shard_map/while
  2186.4 42.9 %all-gather.2.cloned.1.call-done = bf16[128,4096]{1,0:T(8,128)(2,1)} async-done(((bf16[8,4096]{1,0:T(8,128)(2,1)}), bf16[128,4096]{1,0:T(8,128)(2,1)}) %all-gather.2.cloned.1.call-update) | async-done | bytes 1048592 | tf_op jit(solution)/shard_map/while/body/eval_jaxpr/all_gather | solution.py:27
  2229.3 4.8 fusion.46
  2234.1 8.9 fusion.47
  2244.8 88.0 %all-reduce.5.cloned.1.call-done = f32[128,4096]{1,0:T(8,128)} async-done(((f32[128,4096]{1,0:T(8,128)}), f32[128,4096]{1,0:T(8,128)}) %all-reduce.5.cloned.1.call-update) | async-done | bytes 2097168 | tf_op jit(solution)/shard_map/while
  (242 shorter events, 126.9 us)
Async XLA Ops:
  6.6 46.2 %all-gather.2.cloned.1.call-start = ((), (), s32[]{:S(2)}) async-start(), calls=%async_computation | async-start | bytes 1114112 | tf_op jit(solution)/shard_map/while/body/eval_jaxpr/all_gather | solution.py:27
  10.3 146.1 %all-reduce.5.cloned.1.call-start = ((), (), s32[]{:S(2)}) async-start(), calls=%async_computation.1 | async-start | bytes 4194304 | tf_op jit(solution)/shard_map/while
  52.9 4.8 copy-start
  57.6 9.5 copy-start.2
  157.3 4.4 collective-permute-start
  161.7 46.6 %all-gather.2.cloned.1.call-start = ((), (), s32[]{:S(2)}) async-start(), calls=%async_computation | async-start | bytes 1114112 | tf_op jit(solution)/shard_map/while/body/eval_jaxpr/all_gather | solution.py:27
  165.3 146.5 %all-reduce.5.cloned.1.call-start = ((), (), s32[]{:S(2)}) async-start(), calls=%async_computation.1 | async-start | bytes 4194304 | tf_op jit(solution)/shard_map/while
  208.3 4.8 copy-start
  213.1 9.5 copy-start.2
  312.8 4.4 collective-permute-start
  317.2 46.6 %all-gather.2.cloned.1.call-start = ((), (), s32[]{:S(2)}) async-start(), calls=%async_computation | async-start | bytes 1114112 | tf_op jit(solution)/shard_map/while/body/eval_jaxpr/all_gather | solution.py:27
  320.8 146.5 %all-reduce.5.cloned.1.call-start = ((), (), s32[]{:S(2)}) async-start(), calls=%async_computation.1 | async-start | bytes 4194304 | tf_op jit(solution)/shard_map/while
  363.8 4.8 copy-start
  368.6 9.5 copy-start.2
  468.3 4.4 collective-permute-start
  472.7 46.6 %all-gather.2.cloned.1.call-start = ((), (), s32[]{:S(2)}) async-start(), calls=%async_computation | async-start | bytes 1114112 | tf_op jit(solution)/shard_map/while/body/eval_jaxpr/all_gather | solution.py:27
  476.3 146.5 %all-reduce.5.cloned.1.call-start = ((), (), s32[]{:S(2)}) async-start(), calls=%async_computation.1 | async-start | bytes 4194304 | tf_op jit(solution)/shard_map/while
  524.0 9.5 copy-start.2
  623.8 4.4 collective-permute-start
  628.2 46.6 %all-gather.2.cloned.1.call-start = ((), (), s32[]{:S(2)}) async-start(), calls=%async_computation | async-start | bytes 1114112 | tf_op jit(solution)/shard_map/while/body/eval_jaxpr/all_gather | solution.py:27
  631.8 146.5 %all-reduce.5.cloned.1.call-start = ((), (), s32[]{:S(2)}) async-start(), calls=%async_computation.1 | async-start | bytes 4194304 | tf_op jit(solution)/shard_map/while
  679.5 9.5 copy-start.2
  779.2 4.4 collective-permute-start
  783.6 46.6 %all-gather.2.cloned.1.call-start = ((), (), s32[]{:S(2)}) async-start(), calls=%async_computation | async-start | bytes 1114112 | tf_op jit(solution)/shard_map/while/body/eval_jaxpr/all_gather | solution.py:27
  787.3 146.5 %all-reduce.5.cloned.1.call-start = ((), (), s32[]{:S(2)}) async-start(), calls=%async_computation.1 | async-start | bytes 4194304 | tf_op jit(solution)/shard_map/while
  835.0 9.5 copy-start.2
  934.7 4.4 collective-permute-start
  939.1 46.6 %all-gather.2.cloned.1.call-start = ((), (), s32[]{:S(2)}) async-start(), calls=%async_computation | async-start | bytes 1114112 | tf_op jit(solution)/shard_map/while/body/eval_jaxpr/all_gather | solution.py:27
  942.7 146.5 %all-reduce.5.cloned.1.call-start = ((), (), s32[]{:S(2)}) async-start(), calls=%async_computation.1 | async-start | bytes 4194304 | tf_op jit(solution)/shard_map/while
  985.7 4.8 copy-start
  990.5 9.5 copy-start.2
  1090.1 4.4 collective-permute-start
  1094.6 46.6 %all-gather.2.cloned.1.call-start = ((), (), s32[]{:S(2)}) async-start(), calls=%async_computation | async-start | bytes 1114112 | tf_op jit(solution)/shard_map/while/body/eval_jaxpr/all_gather | solution.py:27
  1098.2 146.5 %all-reduce.5.cloned.1.call-start = ((), (), s32[]{:S(2)}) async-start(), calls=%async_computation.1 | async-start | bytes 4194304 | tf_op jit(solution)/shard_map/while
  1145.9 9.5 copy-start.2
  1245.6 4.4 collective-permute-start
  1250.0 46.6 %all-gather.2.cloned.1.call-start = ((), (), s32[]{:S(2)}) async-start(), calls=%async_computation | async-start | bytes 1114112 | tf_op jit(solution)/shard_map/while/body/eval_jaxpr/all_gather | solution.py:27
  1253.6 146.5 %all-reduce.5.cloned.1.call-start = ((), (), s32[]{:S(2)}) async-start(), calls=%async_computation.1 | async-start | bytes 4194304 | tf_op jit(solution)/shard_map/while
  1301.4 9.5 copy-start.2
  1401.0 4.4 collective-permute-start
  1405.5 46.6 %all-gather.2.cloned.1.call-start = ((), (), s32[]{:S(2)}) async-start(), calls=%async_computation | async-start | bytes 1114112 | tf_op jit(solution)/shard_map/while/body/eval_jaxpr/all_gather | solution.py:27
  1409.1 146.5 %all-reduce.5.cloned.1.call-start = ((), (), s32[]{:S(2)}) async-start(), calls=%async_computation.1 | async-start | bytes 4194304 | tf_op jit(solution)/shard_map/while
  1456.8 9.5 copy-start.2
  1556.5 4.4 collective-permute-start
  1560.9 46.6 %all-gather.2.cloned.1.call-start = ((), (), s32[]{:S(2)}) async-start(), calls=%async_computation | async-start | bytes 1114112 | tf_op jit(solution)/shard_map/while/body/eval_jaxpr/all_gather | solution.py:27
  1564.5 146.5 %all-reduce.5.cloned.1.call-start = ((), (), s32[]{:S(2)}) async-start(), calls=%async_computation.1 | async-start | bytes 4194304 | tf_op jit(solution)/shard_map/while
  1612.3 9.5 copy-start.2
  1711.9 4.4 collective-permute-start
  1716.4 46.6 %all-gather.2.cloned.1.call-start = ((), (), s32[]{:S(2)}) async-start(), calls=%async_computation | async-start | bytes 1114112 | tf_op jit(solution)/shard_map/while/body/eval_jaxpr/all_gather | solution.py:27
  1720.0 146.5 %all-reduce.5.cloned.1.call-start = ((), (), s32[]{:S(2)}) async-start(), calls=%async_computation.1 | async-start | bytes 4194304 | tf_op jit(solution)/shard_map/while
  1767.7 9.5 copy-start.2
  1867.4 4.4 collective-permute-start
  1871.8 46.6 %all-gather.2.cloned.1.call-start = ((), (), s32[]{:S(2)}) async-start(), calls=%async_computation | async-start | bytes 1114112 | tf_op jit(solution)/shard_map/while/body/eval_jaxpr/all_gather | solution.py:27
  1875.4 146.5 %all-reduce.5.cloned.1.call-start = ((), (), s32[]{:S(2)}) async-start(), calls=%async_computation.1 | async-start | bytes 4194304 | tf_op jit(solution)/shard_map/while
  1923.2 9.5 copy-start.2
  2022.8 4.4 collective-permute-start
  2027.3 46.6 %all-gather.2.cloned.1.call-start = ((), (), s32[]{:S(2)}) async-start(), calls=%async_computation | async-start | bytes 1114112 | tf_op jit(solution)/shard_map/while/body/eval_jaxpr/all_gather | solution.py:27
  2030.9 146.5 %all-reduce.5.cloned.1.call-start = ((), (), s32[]{:S(2)}) async-start(), calls=%async_computation.1 | async-start | bytes 4194304 | tf_op jit(solution)/shard_map/while
  2078.6 9.5 copy-start.2
  2178.3 4.4 collective-permute-start
  2182.7 46.6 %all-gather.2.cloned.1.call-start = ((), (), s32[]{:S(2)}) async-start(), calls=%async_computation | async-start | bytes 1114112 | tf_op jit(solution)/shard_map/while/body/eval_jaxpr/all_gather | solution.py:27
  2186.3 146.5 %all-reduce.5.cloned.1.call-start = ((), (), s32[]{:S(2)}) async-start(), calls=%async_computation.1 | async-start | bytes 4194304 | tf_op jit(solution)/shard_map/while
  2234.1 9.5 copy-start.2
  2333.7 4.4 collective-permute-start
  (12 other events, 53.4 us)
Sparse Core Ops, SparseCore 0:
  10.4 42.4 all-gather.1
  66.7 89.6 all-reduce.4
  165.4 42.7 all-gather.1
  222.1 89.6 all-reduce.4
  320.9 42.7 all-gather.1
  377.6 89.6 all-reduce.4
  476.4 42.7 all-gather.1
  533.1 89.6 all-reduce.4
  631.9 42.7 all-gather.1
  688.6 89.6 all-reduce.4
  787.4 42.7 all-gather.1
  844.1 89.6 all-reduce.4
  942.8 42.7 all-gather.1
  999.5 89.6 all-reduce.4
  1098.3 42.7 all-gather.1
  1155.0 89.6 all-reduce.4
  1253.7 42.7 all-gather.1
  1310.4 89.6 all-reduce.4
  1409.2 42.7 all-gather.1
  1465.9 89.6 all-reduce.4
  1564.6 42.7 all-gather.1
  1621.3 89.6 all-reduce.4
  1720.1 42.7 all-gather.1
  1776.8 89.6 all-reduce.4
  1875.5 42.7 all-gather.1
  1932.2 89.6 all-reduce.4
  2031.0 42.7 all-gather.1
  2087.7 89.6 all-reduce.4
  2186.4 42.7 all-gather.1
  2243.1 89.6 all-reduce.4
where the time goes:
time: 2350 us
  waiting for transfers between devices  2010 us (86%)
  matrix products  205 us (9%)
  other arithmetic  50.5 us (2%)
  loops' own time  27.9 us (1%)
    while x45, waiting for transfers between devices  1320 us
    all_gather x15, waiting for transfers between devices, apply_layer(): lax.all_gather(normed, 'tensor', axis=0, tiled=True)  643 us
    dot_general x15, matrix products, apply_layer(): jnp.dot(hidden, w_down, preferred_element_type=jnp.float32)  134 us
    dot_general x15, matrix products, swiglu(): gate_out = jnp.dot(normed, w_gate, preferred_element_type=jnp.float32)  71.5 us
  transfers between devices with their start and end apart: 45, of which 45 were waited for; matrix products, arithmetic and copies ran while one was open for 0% of the time, Pallas kernels for 0%

commit v1 on v0

v1 whole, which is shorter than its diff:
```python
import functools

import jax
import jax.numpy as jnp
from jax import lax
from jax.experimental import pallas as pl
from jax.experimental.pallas import tpu as pltpu
from jax.sharding import PartitionSpec as P

MESH = pl.DeviceIdType.MESH
F32 = jnp.float32
BF16 = jnp.bfloat16

SIDE = 4
OWN = 8
CHUNK = SIDE * OWN
PIECE = 512


def kernel(
    stages, blocks, tokens, gain, w_gate_hbm, w_up_hbm, w_down_hbm, states,
    w_gate, w_up, w_down, act_a, act_b, part_a, part_b, sum_a, sum_b, send_a, send_b,
    out_a, out_b, tok_a, tok_b, normed, hidden, fresh, load_sem, recv_sem, send1_sem, send_sem, tok_sem,
):
    stage = lax.axis_index("pipe")
    place = lax.axis_index("tensor")
    x, y = place // SIDE, lax.rem(place, SIDE)
    half = act_a.shape[-1]
    pieces = half // PIECE

    def on(stage_to, x_to, y_to):
        return (stage_to, x_to * SIDE + y_to)

    def turn(value, step):
        return lax.rem(value + step, SIDE)

    loads = [
        pltpu.make_async_copy(source, target, load_sem.at[i])
        for i, (source, target) in enumerate(((w_gate_hbm, w_gate), (w_up_hbm, w_up), (w_down_hbm, w_down)))
    ]
    for load in loads:
        load.start()

    barrier = pltpu.get_barrier_semaphore()
    after, before = lax.rem(stage + 1, stages), lax.rem(stage + stages - 1, stages)
    greeted = 0
    for other in (stage, after, before):
        for step in range(1, SIDE):
            for target in (on(other, turn(x, step), y), on(other, x, turn(y, step))):
                pl.semaphore_signal(barrier, inc=1, device_id=target, device_id_type=MESH)
                greeted += 1
    for other in (after, before):
        pl.semaphore_signal(barrier, inc=1, device_id=on(other, x, y), device_id_type=MESH)
        greeted += 1
    pl.semaphore_wait(barrier, greeted)

    def remote(source, target, sent, received, device):
        return pltpu.make_async_remote_copy(
            src_ref=source, dst_ref=target, send_sem=sent, recv_sem=received, device_id=device, device_id_type=MESH
        )

    def wait_bytes(ref, sem):
        pltpu.make_async_copy(ref, ref, sem).wait()

    def spread_a(i, stage_to):
        for step in range(SIDE):
            remote(out_a.at[i], act_a.at[i, x], send_sem.at[2, i], recv_sem.at[4, i], on(stage_to, turn(x, step), y)).start()

    def spread_b(i, stage_to):
        for step in range(SIDE):
            remote(out_b.at[i], act_b.at[i, y], send_sem.at[3, i], recv_sem.at[5, i], on(stage_to, x, turn(y, step))).start()

    def spread_sent(i):
        wait_bytes(act_a.at[i], send_sem.at[2, i])
        wait_bytes(act_b.at[i], send_sem.at[3, i])

    @pl.when(stage == 1)
    def _():
        for pair in range(blocks // 2):
            rows = jnp.concatenate([tokens[2 * pair].astype(F32), tokens[2 * pair + 1].astype(F32)], axis=0).astype(BF16)
            tok_a[pair, y] = rows[:, :half]
            tok_b[pair, x] = rows[:, half:]
            for step in range(1, SIDE):
                remote(tok_a.at[pair, y], tok_a.at[pair, y], tok_sem.at[0, pair], tok_sem.at[2, pair], on(stage, x, turn(y, step))).start()
                remote(tok_b.at[pair, x], tok_b.at[pair, x], tok_sem.at[1, pair], tok_sem.at[3, pair], on(stage, turn(x, step), y)).start()

        def bring(pair, carry):
            wait_bytes(tok_a.at[pair, pl.ds(0, SIDE - 1)], tok_sem.at[2, pair])
            wait_bytes(tok_b.at[pair, pl.ds(0, SIDE - 1)], tok_sem.at[3, pair])
            for odd in range(2):
                i = 2 * pair + odd
                for tok, out in ((tok_a, out_a), (tok_b, out_b)):
                    out[i] = jnp.concatenate(
                        [tok[pair, k].astype(F32)[odd * OWN : (odd + 1) * OWN] for k in range(SIDE)], axis=0
                    ).astype(BF16)
                spread_a(i, stage - 1)
                spread_b(i, stage - 1)
            return carry

        lax.fori_loop(0, blocks // 2, bring, 0)

        def brought(pair, carry):
            wait_bytes(tok_a.at[pair, pl.ds(0, SIDE - 1)], tok_sem.at[0, pair])
            wait_bytes(tok_b.at[pair, pl.ds(0, SIDE - 1)], tok_sem.at[1, pair])
            for odd in range(2):
                spread_sent(2 * pair + odd)
            return carry

        lax.fori_loop(0, blocks // 2, brought, 0)

    for load in loads:
        load.wait()

    def normalize(i):
        for x_of in range(SIDE):
            for pair in range(SIDE // 2):
                values_a = act_a[i, x_of, 2 * pair * OWN : 2 * (pair + 1) * OWN, :].astype(F32)
                low = x_of // 2 * 2 * OWN
                at = x_of % 2 * OWN
                values_b = jnp.concatenate(
                    [
                        act_b[i, 2 * pair + k, low : low + 2 * OWN, :].astype(F32)[at : at + OWN]
                        for k in range(2)
                    ],
                    axis=0,
                )
                total = jnp.sum(values_a * values_a, axis=-1, keepdims=True) + jnp.sum(values_b * values_b, axis=-1, keepdims=True)
                scale = lax.rsqrt(total * (1.0 / (2 * half)) + 1e-05)
                row = x_of * CHUNK + 2 * pair * OWN
                normed[row : row + 2 * OWN, :half] = (values_a * scale * gain[:, :half]).astype(BF16)
                normed[row : row + 2 * OWN, half:] = (values_b * scale * gain[:, half:]).astype(BF16)

    def compute(i):
        slot = lax.rem(i, 2)
        wait_bytes(act_a.at[i], recv_sem.at[4, i])
        wait_bytes(act_b.at[i], recv_sem.at[5, i])
        normalize(i)
        gate = jnp.dot(normed[...], w_gate[...], preferred_element_type=F32)
        up = jnp.dot(normed[...], w_up[...], preferred_element_type=F32)
        hidden[...] = (gate / (1.0 + jnp.exp(-gate)) * up).astype(BF16)

        @pl.when(i >= 2)
        def _():
            wait_bytes(send_a.at[slot, pl.ds(0, SIDE - 1)], send1_sem.at[0, slot])
            wait_bytes(send_b.at[slot, pl.ds(0, SIDE - 1)], send1_sem.at[1, slot])

        def down_a(piece, carry):
            at = pl.ds(pl.multiple_of(piece * PIECE, PIECE), PIECE)
            share = jnp.dot(hidden[...], w_down[:, at], preferred_element_type=F32)
            for k in range(SIDE):
                send_a[slot, k, :, at] = share[k * CHUNK : (k + 1) * CHUNK].astype(BF16)
            return carry

        lax.fori_loop(0, pieces, down_a, 0)
        for step in range(1, SIDE):
            to = turn(x, step)
            remote(send_a.at[slot, to], part_a.at[i, step - 1], send1_sem.at[0, slot], recv_sem.at[0, i], on(stage, to, y)).start()

        def down_b(piece, carry):
            at = pl.ds(pl.multiple_of(piece * PIECE, PIECE), PIECE)
            from_w = pl.ds(pl.multiple_of(piece * PIECE + half, PIECE), PIECE)
            share = jnp.dot(hidden[...], w_down[:, from_w], preferred_element_type=F32)
            for k in range(SIDE):
                rows = [share[m * CHUNK + k * OWN : m * CHUNK + (k + 1) * OWN] for m in range(SIDE)]
                send_b[slot, k, :, at] = jnp.concatenate(rows, axis=0).astype(BF16)
            return carry

        lax.fori_loop(0, pieces, down_b, 0)
        for step in range(1, SIDE):
            to = turn(y, step)
            remote(send_b.at[slot, to], part_b.at[i, step - 1], send1_sem.at[1, slot], recv_sem.at[1, i], on(stage, x, to)).start()

    def reduce_line(i):
        slot = lax.rem(i, 2)

        def add(send, mine, part, total, entry):
            def one(piece, carry):
                at = pl.ds(pl.multiple_of(piece * PIECE, PIECE), PIECE)
                value = send[slot, mine, :, at].astype(F32)
                for k in range(SIDE - 1):
                    value += part[i, k, :, at].astype(F32)
                total[i, entry, :, at] = value.astype(BF16)
                return carry

            lax.fori_loop(0, pieces, one, 0)

        wait_bytes(part_a.at[i], recv_sem.at[0, i])
        add(send_a, x, part_a, sum_a, y)
        for step in range(1, SIDE):
            remote(sum_a.at[i, y], sum_a.at[i, y], send_sem.at[0, i], recv_sem.at[2, i], on(stage, x, turn(y, step))).start()
        wait_bytes(part_b.at[i], recv_sem.at[1, i])
        add(send_b, y, part_b, sum_b, x)
        for step in range(1, SIDE):
            remote(sum_b.at[i, x], sum_b.at[i, x], send_sem.at[1, i], recv_sem.at[3, i], on(stage, turn(x, step), y)).start()

    def finish(i):
        def add(act, mine, total, out, own_at, column):
            def one(piece, carry):
                at = pl.ds(pl.multiple_of(piece * PIECE, PIECE), PIECE)
                branch = total[i, 0, :, at].astype(F32)
                for k in range(1, SIDE):
                    branch += total[i, k, :, at].astype(F32)
                value = act[i, mine, :, at].astype(F32) + branch
                out[i, :, at] = value.astype(BF16)
                fresh[:, at] = value
                return carry

            lax.fori_loop(0, pieces, one, 0)
            own = fresh[pl.ds(pl.multiple_of(own_at * OWN, OWN), OWN), :]
            states[i, :, column : column + half] = own.astype(BF16)

        wait_bytes(sum_a.at[i, pl.ds(0, SIDE - 1)], recv_sem.at[2, i])
        add(act_a, x, sum_a, out_a, y, 0)

        @pl.when(stage < stages - 1)
        def _():
            spread_a(i, stage + 1)

        wait_bytes(sum_b.at[i, pl.ds(0, SIDE - 1)], recv_sem.at[3, i])
        add(act_b, y, sum_b, out_b, x, half)

        @pl.when(stage < stages - 1)
        def _():
            spread_b(i, stage + 1)

    def advance(i, carry):
        compute(i)

        @pl.when(i > 0)
        def _():
            finish(i - 1)

        reduce_line(i)
        return carry

    lax.fori_loop(0, blocks, advance, 0)
    finish(blocks - 1)

    def drain(i, carry):
        wait_bytes(sum_a.at[i, pl.ds(0, SIDE - 1)], send_sem.at[0, i])
        wait_bytes(sum_b.at[i, pl.ds(0, SIDE - 1)], send_sem.at[1, i])

        @pl.when(stage < stages - 1)
        def _():
            spread_sent(i)

        return carry

    lax.fori_loop(0, blocks, drain, 0)
    for slot in range(2):
        wait_bytes(send_a.at[slot, pl.ds(0, SIDE - 1)], send1_sem.at[0, slot])
        wait_bytes(send_b.at[slot, pl.ds(0, SIDE - 1)], send1_sem.at[1, slot])


def solution(mesh):
    stages = mesh.shape["pipe"]

    def local(tokens, norm_gain, gate_weight, up_weight, down_weight):
        blocks, _, width = tokens.shape
        units = gate_weight.shape[2]
        half = width // 2
        vmem = pl.BlockSpec(memory_space=pltpu.VMEM)
        hbm = pl.BlockSpec(memory_space=pl.ANY)
        dma = pltpu.SemaphoreType.DMA
        states = pl.pallas_call(
            functools.partial(kernel, stages, blocks),
            out_shape=jax.ShapeDtypeStruct(tokens.shape, BF16),
            in_specs=[vmem, vmem, hbm, hbm, hbm],
            out_specs=vmem,
            scratch_shapes=[
                pltpu.VMEM((width, units), BF16),
                pltpu.VMEM((width, units), BF16),
                pltpu.VMEM((units, width), BF16),
                pltpu.VMEM((blocks, SIDE, CHUNK, half), BF16),
                pltpu.VMEM((blocks, SIDE, CHUNK, half), BF16),
                pltpu.VMEM((blocks, SIDE - 1, CHUNK, half), BF16),
                pltpu.VMEM((blocks, SIDE - 1, CHUNK, half), BF16),
                pltpu.VMEM((blocks, SIDE, CHUNK, half), BF16),
                pltpu.VMEM((blocks, SIDE, CHUNK, half), BF16),
                pltpu.VMEM((2, SIDE, CHUNK, half), BF16),
                pltpu.VMEM((2, SIDE, CHUNK, half), BF16),
                pltpu.VMEM((blocks, CHUNK, half), BF16),
                pltpu.VMEM((blocks, CHUNK, half), BF16),
                pltpu.VMEM((blocks // 2, SIDE, 2 * OWN, half), BF16),
                pltpu.VMEM((blocks // 2, SIDE, 2 * OWN, half), BF16),
                pltpu.VMEM((SIDE * CHUNK, width), BF16),
                pltpu.VMEM((SIDE * CHUNK, units), BF16),
                pltpu.VMEM((CHUNK, half), F32),
                dma((3,)),
                dma((6, blocks)),
                dma((2, 2)),
                dma((4, blocks)),
                dma((4, blocks // 2)),
            ],
            compiler_params=pltpu.CompilerParams(
                collective_id=0, has_side_effects=True, vmem_limit_bytes=62 * 2**20
            ),
            cost_estimate=pl.CostEstimate(
                flops=2 * 3 * blocks * SIDE * CHUNK * width * units,
                bytes_accessed=6 * width * units,
                transcendentals=blocks * SIDE * CHUNK * units,
            ),
        )(tokens, norm_gain, gate_weight[0], up_weight[0], down_weight[0])
        return states[None]

    in_specs = (
        P(None, "tensor", None),
        P("pipe", None),
        P("pipe", None, "tensor"),
        P("pipe", None, "tensor"),
        P("pipe", "tensor", None),
    )
    out_specs = P("pipe", None, "tensor", None)
    return jax.shard_map(local, mesh=mesh, in_specs=in_specs, out_specs=out_specs, check_vma=False)
```

time: 2350 us -> 403 us (0.17)
  waiting for transfers between devices: 2010 us -> 0 us
  Pallas kernels: 0 us -> 401 us
  matrix products: 205 us -> 0 us
  other arithmetic: 50.5 us -> 0 us
  loops' own time: 27.9 us -> 0 us
    while x45 -> x0, waiting for transfers between devices: 1320 us -> none
    all_gather x15 -> x0, waiting for transfers between devices: 643 us -> none  [apply_layer(): lax.all_gather(normed, 'tensor', axis=0, tiled=True)]
    pallas_call x0 -> x1, Pallas kernels: none -> 401 us  [local(): pl.pallas_call(functools.partial(kernel, stages, blocks), out_shape=jax.S...]
    dot_general x30 -> x0, matrix products: 205 us -> none  [the longest x15 134 us: apply_layer(): jnp.dot(hidden, w_down, preferred_element_type=jnp.float32)]
    ppermute x15 -> x0, waiting for transfers between devices: 46.8 us -> none  [passed_along(): lax.ppermute(value, axis, [(source, source + steps) for source in range(l...]
    another operation x1 -> x0, loops' own time: 27.9 us -> none  [local(): lax.scan(advance, (start_rows, start_states), ticks_all)]
  transfers between devices with their start and end apart: 45 -> 0, of which waited for: 45 -> 0; matrix products, arithmetic and copies ran while one was open for 0% -> 0% of each run, Pallas kernels for 0% -> 0%
where the time goes in v1:
time: 403 us
  Pallas kernels  401 us (100%)
    pallas_call x1, Pallas kernels, local(): pl.pallas_call(functools.partial(kernel, stages, blocks), out_shape=jax.S...  401 us

profile of v1, /device:TPU:97, one launch (start us, length us, event | category | flops | bytes accessed | tf_op | source)
XLA Modules:
  0.0 402.8 jit_solution(4996655194669424114)
XLA Ops:
  0.0 400.9 %shard_map.55 = bf16[8,8,4096]{2,1,0:T(8,128)(2,1)} custom-call(bf16[8,8,4096]{2,1,0:T(8,128)(2,1)} %tokens.1, f32[1,4096]{1,0:T(1,128)} %gain.1, bf16[4096,896]{1,0:T(8,128)(2,1)} %bitcast.5, bf16[4096,896]{1,0:T(8,128)(2,1)} %bitcast.6, bf16[896,4096]{1,0:T(8,128)(2,1)} %bitcast.7), custom_call_target="tpu_custom_call" | custom-call | flops 22548578304 | bytes 22020096 | tf_op jit(solution)/shard_map/pallas_call | solution.py:265
  400.9 1.9 copy.7

commit v2 on v1

v2 whole, which is shorter than its diff:
```python
import functools

import jax
import jax.numpy as jnp
from jax import lax
from jax.experimental import pallas as pl
from jax.experimental.pallas import tpu as pltpu
from jax.sharding import PartitionSpec as P

MESH = pl.DeviceIdType.MESH
F32 = jnp.float32
BF16 = jnp.bfloat16

SIDE = 4
OWN = 8
CHUNK = SIDE // 2 * OWN
PIECE = 1024
ORDER = (("down", 0), ("finish", 1), ("up", -1), ("line", 0))


def kernel(
    stages, blocks, tokens, gain, w_gate_hbm, w_up_hbm, w_down_hbm, states,
    w_gate, w_up, w_down, act_a, act_b, part_a, part_b, sum_a, sum_b, send_a, send_b,
    out_a, out_b, tok_a, tok_b, gate_sum, up_sum, squares, hidden, fresh, load_sem, recv_sem, send1_sem, send_sem, tok_sem,
):
    stage = lax.axis_index("pipe")
    place = lax.axis_index("tensor")
    x, y = place // SIDE, lax.rem(place, SIDE)
    pieces = act_a.shape[1]
    half = pieces * PIECE
    pairs = blocks // 4

    def on(stage_to, x_to, y_to):
        return (stage_to, x_to * SIDE + y_to)

    def turn(value, step):
        return lax.rem(value + step, SIDE)

    loads = []
    for p in range(pieces):
        for k in range(2):
            for j, (source, target) in enumerate(((w_gate_hbm, w_gate), (w_up_hbm, w_up))):
                loads.append(
                    pltpu.make_async_copy(
                        source.at[pl.ds(k * half + p * PIECE, PIECE)],
                        target.at[p, pl.ds(k * PIECE, PIECE)],
                        load_sem.at[(p * 2 + k) * 2 + j],
                    )
                )
    loads.append(pltpu.make_async_copy(w_down_hbm, w_down, load_sem.at[4 * pieces]))
    for load in loads:
        load.start()

    barrier = pltpu.get_barrier_semaphore()
    after, before = lax.rem(stage + 1, stages), lax.rem(stage + stages - 1, stages)
    greeted = 0
    for other in (stage, after, before):
        for step in range(1, SIDE):
            for target in (on(other, turn(x, step), y), on(other, x, turn(y, step))):
                pl.semaphore_signal(barrier, inc=1, device_id=target, device_id_type=MESH)
                greeted += 1
    for other in (after, before):
        pl.semaphore_signal(barrier, inc=1, device_id=on(other, x, y), device_id_type=MESH)
        greeted += 1
    pl.semaphore_wait(barrier, greeted)

    def remote(source, target, sent, received, device):
        return pltpu.make_async_remote_copy(
            src_ref=source, dst_ref=target, send_sem=sent, recv_sem=received, device_id=device, device_id_type=MESH
        )

    def wait_bytes(ref, sem):
        pltpu.make_async_copy(ref, ref, sem).wait()

    def spread_a(i, p, stage_to):
        for step in range(SIDE):
            remote(out_a.at[i, p], act_a.at[i, p, x], send_sem.at[2, i], recv_sem.at[4, i, p], on(stage_to, turn(x, step), y)).start()

    def spread_b(i, p, stage_to):
        for step in range(SIDE):
            remote(out_b.at[i, p], act_b.at[i, p, y], send_sem.at[3, i], recv_sem.at[5, i, p], on(stage_to, x, turn(y, step))).start()

    def spread_sent(i):
        wait_bytes(act_a.at[i], send_sem.at[2, i])
        wait_bytes(act_b.at[i], send_sem.at[3, i])

    @pl.when(stage == 1)
    def _():
        for pair in range(pairs):
            rows = jnp.concatenate([tokens[2 * pair].astype(F32), tokens[2 * pair + 1].astype(F32)], axis=0).astype(BF16)
            tok_a[pair, y] = rows[:, :half]
            tok_b[pair, x] = rows[:, half:]
            for step in range(1, SIDE):
                remote(tok_a.at[pair, y], tok_a.at[pair, y], tok_sem.at[0, pair], tok_sem.at[2, pair], on(stage, x, turn(y, step))).start()
                remote(tok_b.at[pair, x], tok_b.at[pair, x], tok_sem.at[1, pair], tok_sem.at[3, pair], on(stage, turn(x, step), y)).start()

        def bring(pair, carry):
            wait_bytes(tok_a.at[pair, pl.ds(0, SIDE - 1)], tok_sem.at[2, pair])
            wait_bytes(tok_b.at[pair, pl.ds(0, SIDE - 1)], tok_sem.at[3, pair])
            for half_of_pair in range(2):
                for parity in range(2):
                    i = 4 * pair + 2 * half_of_pair + parity
                    for p in range(pieces):
                        at = slice(p * PIECE, (p + 1) * PIECE)
                        own = slice(half_of_pair * OWN, (half_of_pair + 1) * OWN)
                        for tok, out, mine in ((tok_a, out_a, x), (tok_b, out_b, y)):
                            first = lax.rem(mine + parity, 2)
                            out[i, p] = jnp.concatenate(
                                [tok[pair, first + 2 * k, :, at].astype(F32)[own] for k in range(SIDE // 2)], axis=0
                            ).astype(BF16)
                        spread_a(i, p, stage - 1)
                        spread_b(i, p, stage - 1)
            return carry

        lax.fori_loop(0, pairs, bring, 0)

        def brought(pair, carry):
            wait_bytes(tok_a.at[pair, pl.ds(0, SIDE - 1)], tok_sem.at[0, pair])
            wait_bytes(tok_b.at[pair, pl.ds(0, SIDE - 1)], tok_sem.at[1, pair])
            for k in range(4):
                spread_sent(4 * pair + k)
            return carry

        lax.fori_loop(0, pairs, brought, 0)

    for load in loads:
        load.wait()

    def up(i):
        rows = SIDE * CHUNK
        parity = lax.rem(i, 2)

        for p in range(pieces):
            wait_bytes(act_a.at[i, p], recv_sem.at[4, i, p])
            wait_bytes(act_b.at[i, p], recv_sem.at[5, i, p])
            values_a = act_a[i, p].astype(F32).reshape(rows, PIECE)
            even = [act_b[i, p, 2 * j + parity].astype(F32) for j in range(SIDE // 2)]
            odd = [act_b[i, p, 2 * j + 1 - parity].astype(F32) for j in range(SIDE // 2)]
            values_b = jnp.concatenate(
                [
                    (odd if m % 2 else even)[j][m // 2 * OWN : (m // 2 + 1) * OWN]
                    for m in range(SIDE)
                    for j in range(SIDE // 2)
                ],
                axis=0,
            )
            square = jnp.zeros((rows, 128), F32)
            for values in (values_a, values_b):
                for lane in range(0, PIECE, 128):
                    part = values[:, lane : lane + 128]
                    square += part * part
            scaled = jnp.concatenate(
                [
                    (values_a * gain[:, p * PIECE : (p + 1) * PIECE]).astype(BF16),
                    (values_b * gain[:, half + p * PIECE : half + (p + 1) * PIECE]).astype(BF16),
                ],
                axis=1,
            )
            gate = jnp.dot(scaled, w_gate[p], preferred_element_type=F32)
            up = jnp.dot(scaled, w_up[p], preferred_element_type=F32)
            if p == 0:
                squares[...] = square
                gate_sum[...] = gate
                up_sum[...] = up
            else:
                squares[...] += square
                gate_sum[...] += gate
                up_sum[...] += up
        mean = jnp.sum(squares[...], axis=-1, keepdims=True) * (1.0 / (2 * half))
        scale = lax.rsqrt(mean + 1e-05)
        gate = gate_sum[...] * scale
        hidden[...] = (gate / (1.0 + jnp.exp(-gate)) * (up_sum[...] * scale)).astype(BF16)

    def down(i):
        slot = lax.rem(i, 2)
        parity = lax.rem(i, 2)

        @pl.when(i >= 2)
        def _():
            sent_line(slot)

        def one(p, carry):
            share = jnp.dot(
                hidden[...], w_down[:, pl.ds(pl.multiple_of(p * PIECE, PIECE), PIECE)], preferred_element_type=F32
            )
            for k in range(SIDE):
                send_a[slot, p, k] = share[k * CHUNK : (k + 1) * CHUNK].astype(BF16)
            for step in range(1, SIDE):
                to = turn(x, step)
                remote(send_a.at[slot, p, to], part_a.at[i, p, step - 1], send1_sem.at[0, slot], recv_sem.at[0, i, p], on(stage, to, y)).start()
            share = jnp.dot(
                hidden[...], w_down[:, pl.ds(pl.multiple_of(half + p * PIECE, PIECE), PIECE)], preferred_element_type=F32
            )
            for j in range(SIDE // 2):
                groups = [share[m * CHUNK + j * OWN : m * CHUNK + (j + 1) * OWN] for m in range(SIDE)]
                send_b[slot, p, 2 * j + parity] = jnp.concatenate(groups[0::2], axis=0).astype(BF16)
                send_b[slot, p, 2 * j + 1 - parity] = jnp.concatenate(groups[1::2], axis=0).astype(BF16)
            for step in range(1, SIDE):
                to = turn(y, step)
                remote(send_b.at[slot, p, to], part_b.at[i, p, step - 1], send1_sem.at[1, slot], recv_sem.at[1, i, p], on(stage, x, to)).start()
            return carry

        lax.fori_loop(0, pieces, one, 0)

    def sent_line(slot):
        wait_bytes(send_a.at[slot, :, pl.ds(0, SIDE - 1)], send1_sem.at[0, slot])
        wait_bytes(send_b.at[slot, :, pl.ds(0, SIDE - 1)], send1_sem.at[1, slot])

    def reduce_line(i):
        slot = lax.rem(i, 2)

        def add(p, send, mine, part, total, entry):
            value = send[slot, p, mine].astype(F32)
            for k in range(SIDE - 1):
                value += part[i, p, k].astype(F32)
            total[i, p, entry] = value.astype(BF16)

        def one(p, carry):
            wait_bytes(part_a.at[i, p], recv_sem.at[0, i, p])
            add(p, send_a, x, part_a, sum_a, y)
            for step in range(1, SIDE):
                remote(sum_a.at[i, p, y], sum_a.at[i, p, y], send_sem.at[0, i], recv_sem.at[2, i, p], on(stage, x, turn(y, step))).start()
            wait_bytes(part_b.at[i, p], recv_sem.at[1, i, p])
            add(p, send_b, y, part_b, sum_b, x)
            for step in range(1, SIDE):
                remote(sum_b.at[i, p, x], sum_b.at[i, p, x], send_sem.at[1, i], recv_sem.at[3, i, p], on(stage, turn(x, step), y)).start()
            return carry

        lax.fori_loop(0, pieces, one, 0)

    def finish(i):
        def add(p, act, mine, total, out, own_at, column):
            branch = total[i, p, 0].astype(F32)
            for k in range(1, SIDE):
                branch += total[i, p, k].astype(F32)
            value = act[i, p, mine].astype(F32) + branch
            out[i, p] = value.astype(BF16)

            @pl.when(lax.rem(x + y + i, 2) == 0)
            def _():
                fresh[...] = value
                own = fresh[pl.ds(pl.multiple_of(own_at // 2 * OWN, OWN), OWN), :]
                states[i // 2, :, pl.ds(pl.multiple_of(column + p * PIECE, PIECE), PIECE)] = own.astype(BF16)

        def one(p, carry):
            wait_bytes(sum_a.at[i, p, pl.ds(0, SIDE - 1)], recv_sem.at[2, i, p])
            add(p, act_a, x, sum_a, out_a, y, 0)

            @pl.when(stage < stages - 1)
            def _():
                spread_a(i, p, stage + 1)

            wait_bytes(sum_b.at[i, p, pl.ds(0, SIDE - 1)], recv_sem.at[3, i, p])
            add(p, act_b, y, sum_b, out_b, x, half)

            @pl.when(stage < stages - 1)
            def _():
                spread_b(i, p, stage + 1)

            return carry

        lax.fori_loop(0, pieces, one, 0)

    work = {"up": up, "down": down, "line": reduce_line, "finish": finish}

    def advance(step, carry):
        for name, lag in ORDER:
            i = step - lag

            @pl.when((i >= 0) & (i < blocks))
            def _(name=name, i=i):
                work[name](i)

        return carry

    lags = [lag for _, lag in ORDER]
    lax.fori_loop(min(lags), blocks + max(lags), advance, 0)

    def drain(i, carry):
        wait_bytes(sum_a.at[i, :, pl.ds(0, SIDE - 1)], send_sem.at[0, i])
        wait_bytes(sum_b.at[i, :, pl.ds(0, SIDE - 1)], send_sem.at[1, i])

        @pl.when(stage < stages - 1)
        def _():
            spread_sent(i)

        return carry

    lax.fori_loop(0, blocks, drain, 0)
    for slot in range(2):
        sent_line(slot)


def solution(mesh):
    stages = mesh.shape["pipe"]

    def local(tokens, norm_gain, gate_weight, up_weight, down_weight):
        blocks, _, width = tokens.shape
        blocks *= 2
        units = gate_weight.shape[2]
        half = width // 2
        pieces = half // PIECE
        vmem = pl.BlockSpec(memory_space=pltpu.VMEM)
        hbm = pl.BlockSpec(memory_space=pl.ANY)
        dma = pltpu.SemaphoreType.DMA
        states = pl.pallas_call(
            functools.partial(kernel, stages, blocks),
            out_shape=jax.ShapeDtypeStruct(tokens.shape, BF16),
            in_specs=[vmem, vmem, hbm, hbm, hbm],
            out_specs=vmem,
            scratch_shapes=[
                pltpu.VMEM((pieces, 2 * PIECE, units), BF16),
                pltpu.VMEM((pieces, 2 * PIECE, units), BF16),
                pltpu.VMEM((units, width), BF16),
                pltpu.VMEM((blocks, pieces, SIDE, CHUNK, PIECE), BF16),
                pltpu.VMEM((blocks, pieces, SIDE, CHUNK, PIECE), BF16),
                pltpu.VMEM((blocks, pieces, SIDE - 1, CHUNK, PIECE), BF16),
                pltpu.VMEM((blocks, pieces, SIDE - 1, CHUNK, PIECE), BF16),
                pltpu.VMEM((blocks, pieces, SIDE, CHUNK, PIECE), BF16),
                pltpu.VMEM((blocks, pieces, SIDE, CHUNK, PIECE), BF16),
                pltpu.VMEM((2, pieces, SIDE, CHUNK, PIECE), BF16),
                pltpu.VMEM((2, pieces, SIDE, CHUNK, PIECE), BF16),
                pltpu.VMEM((blocks, pieces, CHUNK, PIECE), BF16),
                pltpu.VMEM((blocks, pieces, CHUNK, PIECE), BF16),
                pltpu.VMEM((blocks // 4, SIDE, 2 * OWN, half), BF16),
                pltpu.VMEM((blocks // 4, SIDE, 2 * OWN, half), BF16),
                pltpu.VMEM((SIDE * CHUNK, units), F32),
                pltpu.VMEM((SIDE * CHUNK, units), F32),
                pltpu.VMEM((SIDE * CHUNK, 128), F32),
                pltpu.VMEM((SIDE * CHUNK, units), BF16),
                pltpu.VMEM((CHUNK, PIECE), F32),
                dma((4 * pieces + 1,)),
                dma((6, blocks, pieces)),
                dma((2, 2)),
                dma((4, blocks)),
                dma((4, blocks // 4)),
            ],
            compiler_params=pltpu.CompilerParams(
                collective_id=0, has_side_effects=True, vmem_limit_bytes=62 * 2**20
            ),
            cost_estimate=pl.CostEstimate(
                flops=2 * 3 * blocks * SIDE * CHUNK * width * units,
                bytes_accessed=6 * width * units,
                transcendentals=blocks * SIDE * CHUNK * units,
            ),
        )(tokens, norm_gain, gate_weight[0], up_weight[0], down_weight[0])
        return states[None]

    in_specs = (
        P(None, "tensor", None),
        P("pipe", None),
        P("pipe", None, "tensor"),
        P("pipe", None, "tensor"),
        P("pipe", "tensor", None),
    )
    out_specs = P("pipe", None, "tensor", None)
    return jax.shard_map(local, mesh=mesh, in_specs=in_specs, out_specs=out_specs, check_vma=False)
```

time: 403 us -> 316 us (0.78)
  Pallas kernels: 401 us -> 314 us
    pallas_call x1, Pallas kernels: 401 us -> 314 us  [local(): pl.pallas_call(functools.partial(kernel, stages, blocks), out_shape=jax.S...]
where the time goes in v2:
time: 316 us
  Pallas kernels  314 us (99%)
    pallas_call x1, Pallas kernels, local(): pl.pallas_call(functools.partial(kernel, stages, blocks), out_shape=jax.S...  314 us

profile of v2, /device:TPU:97, one launch (start us, length us, event | category | flops | bytes accessed | tf_op | source)
XLA Modules:
  0.0 315.6 jit_solution(9001237847001742938)
XLA Ops:
  0.0 313.8 %shard_map.55 = bf16[8,8,4096]{2,1,0:T(8,128)(2,1)} custom-call(bf16[8,8,4096]{2,1,0:T(8,128)(2,1)} %tokens.1, f32[1,4096]{1,0:T(1,128)} %gain.1, bf16[4096,896]{1,0:T(8,128)(2,1)} %bitcast.5, bf16[4096,896]{1,0:T(8,128)(2,1)} %bitcast.6, bf16[896,4096]{1,0:T(8,128)(2,1)} %bitcast.7), custom_call_target="tpu_custom_call" | custom-call | flops 22548578304 | bytes 22020096 | tf_op jit(solution)/shard_map/pallas_call | solution.py:306
  313.8 1.9 copy.7

commit v3 on v2

--- a/solution.py
+++ b/solution.py
@@ -14,8 +14,20 @@
 SIDE = 4
 OWN = 8
 CHUNK = SIDE // 2 * OWN
-PIECE = 1024
-ORDER = (("down", 0), ("finish", 1), ("up", -1), ("line", 0))
+PIECE = 512
+ORDER = (
+    ("down", 0, 0, 2),
+    ("finish", 1, 0, 1),
+    ("down", 0, 2, 4),
+    ("finish", 1, 1, 3),
+    ("up", -1, 0, 2),
+    ("line", 0, 0, 1),
+    ("finish", 1, 3, 4),
+    ("line", 0, 1, 2),
+    ("up", -1, 2, 3),
+    ("line", 0, 2, 4),
+    ("up", -1, 3, 4),
+)
 
 
 def kernel(
@@ -53,15 +65,14 @@
 
     barrier = pltpu.get_barrier_semaphore()
     after, before = lax.rem(stage + 1, stages), lax.rem(stage + stages - 1, stages)
-    greeted = 0
-    for other in (stage, after, before):
+    source = jnp.where(stage == 0, after, before)
+    for other in (stage, source):
         for step in range(1, SIDE):
             for target in (on(other, turn(x, step), y), on(other, x, turn(y, step))):
                 pl.semaphore_signal(barrier, inc=1, device_id=target, device_id_type=MESH)
-                greeted += 1
-    for other in (after, before):
-        pl.semaphore_signal(barrier, inc=1, device_id=on(other, x, y), device_id_type=MESH)
-        greeted += 1
+    pl.semaphore_signal(barrier, inc=1, device_id=on(source, x, y), device_id_type=MESH)
+    line = 2 * (SIDE - 1)
+    greeted = line + jnp.where(stage == stages - 1, 0, line + 1) + jnp.where(stage == 1, line + 1, 0)
     pl.semaphore_wait(barrier, greeted)
 
     def remote(source, target, sent, received, device):
@@ -126,11 +137,11 @@
     for load in loads:
         load.wait()
 
-    def up(i):
+    def up(i, first, last):
         rows = SIDE * CHUNK
         parity = lax.rem(i, 2)
 
-        for p in range(pieces):
+        for p in range(first, last):
             wait_bytes(act_a.at[i, p], recv_sem.at[4, i, p])
             wait_bytes(act_b.at[i, p], recv_sem.at[5, i, p])
             values_a = act_a[i, p].astype(F32).reshape(rows, PIECE)
@@ -166,18 +177,21 @@
                 squares[...] += square
                 gate_sum[...] += gate
                 up_sum[...] += up
-        mean = jnp.sum(squares[...], axis=-1, keepdims=True) * (1.0 / (2 * half))
-        scale = lax.rsqrt(mean + 1e-05)
-        gate = gate_sum[...] * scale
-        hidden[...] = (gate / (1.0 + jnp.exp(-gate)) * (up_sum[...] * scale)).astype(BF16)
-
-    def down(i):
+        if last == pieces:
+            mean = jnp.sum(squares[...], axis=-1, keepdims=True) * (1.0 / (2 * half))
+            scale = lax.rsqrt(mean + 1e-05)
+            gate = gate_sum[...] * scale
+            hidden[...] = (gate / (1.0 + jnp.exp(-gate)) * (up_sum[...] * scale)).astype(BF16)
+
+    def down(i, first, last):
         slot = lax.rem(i, 2)
         parity = lax.rem(i, 2)
 
-        @pl.when(i >= 2)
-        def _():
-            sent_line(slot)
+        if first == 0:
+
+            @pl.when(i >= 2)
+            def _():
+                sent_line(slot)
 
         def one(p, carry):
             share = jnp.dot(
@@ -200,13 +214,13 @@
                 remote(send_b.at[slot, p, to], part_b.at[i, p, step - 1], send1_sem.at[1, slot], recv_sem.at[1, i, p], on(stage, x, to)).start()
             return carry
 
-        lax.fori_loop(0, pieces, one, 0)
+        lax.fori_loop(first, last, one, 0)
 
     def sent_line(slot):
         wait_bytes(send_a.at[slot, :, pl.ds(0, SIDE - 1)], send1_sem.at[0, slot])
         wait_bytes(send_b.at[slot, :, pl.ds(0, SIDE - 1)], send1_sem.at[1, slot])
 
-    def reduce_line(i):
+    def reduce_line(i, first, last):
         slot = lax.rem(i, 2)
 
         def add(p, send, mine, part, total, entry):
@@ -226,9 +240,9 @@
                 remote(sum_b.at[i, p, x], sum_b.at[i, p, x], send_sem.at[1, i], recv_sem.at[3, i, p], on(stage, turn(x, step), y)).start()
             return carry
 
-        lax.fori_loop(0, pieces, one, 0)
-
-    def finish(i):
+        lax.fori_loop(first, last, one, 0)
+
+    def finish(i, first, last):
         def add(p, act, mine, total, out, own_at, column):
             branch = total[i, p, 0].astype(F32)
             for k in range(1, SIDE):
@@ -259,21 +273,21 @@
 
             return carry
 
-        lax.fori_loop(0, pieces, one, 0)
+        lax.fori_loop(first, last, one, 0)
 
     work = {"up": up, "down": down, "line": reduce_line, "finish": finish}
 
     def advance(step, carry):
-        for name, lag in ORDER:
+        for name, lag, first, last in ORDER:
             i = step - lag
 
             @pl.when((i >= 0) & (i < blocks))
-            def _(name=name, i=i):
-                work[name](i)
+            def _(name=name, i=i, first=first, last=last):
+                work[name](i, first, last)
 
         return carry
 
-    lags = [lag for _, lag in ORDER]
+    lags = [entry[1] for entry in ORDER]
     lax.fori_loop(min(lags), blocks + max(lags), advance, 0)
 
     def drain(i, carry):

time: 316 us -> 305 us (0.965)
  Pallas kernels: 314 us -> 303 us
    pallas_call x1, Pallas kernels: 314 us -> 303 us  [local(): pl.pallas_call(functools.partial(kernel, stages, blocks), out_shape=jax.S...]
where the time goes in v3:
time: 305 us
  Pallas kernels  303 us (99%)
    pallas_call x1, Pallas kernels, local(): pl.pallas_call(functools.partial(kernel, stages, blocks), out_shape=jax.S...  303 us

profile of v3, /device:TPU:97, one launch (start us, length us, event | category | flops | bytes accessed | tf_op | source)
XLA Modules:
  0.0 304.9 jit_solution(6913669422520201428)
XLA Ops:
  0.0 303.1 %shard_map.55 = bf16[8,8,4096]{2,1,0:T(8,128)(2,1)} custom-call(bf16[8,8,4096]{2,1,0:T(8,128)(2,1)} %tokens.1, f32[1,4096]{1,0:T(1,128)} %gain.1, bf16[4096,896]{1,0:T(8,128)(2,1)} %bitcast.5, bf16[4096,896]{1,0:T(8,128)(2,1)} %bitcast.6, bf16[896,4096]{1,0:T(8,128)(2,1)} %bitcast.7), custom_call_target="tpu_custom_call" | custom-call | flops 22548578304 | bytes 22020096 | tf_op jit(solution)/shard_map/pallas_call | solution.py:320
  303.1 1.9 copy.7

commit v4 on v3

--- a/solution.py
+++ b/solution.py
@@ -28,6 +28,7 @@
     ("line", 0, 2, 4),
     ("up", -1, 3, 4),
 )
+NEAR = 6
 
 
 def kernel(
@@ -65,14 +66,20 @@
 
     barrier = pltpu.get_barrier_semaphore()
     after, before = lax.rem(stage + 1, stages), lax.rem(stage + stages - 1, stages)
-    source = jnp.where(stage == 0, after, before)
-    for other in (stage, source):
-        for step in range(1, SIDE):
-            for target in (on(other, turn(x, step), y), on(other, x, turn(y, step))):
+    def greet(other, steps):
+        for step in steps:
+            for target in (on(other, turn(x, step), y), on(other, x, turn(y, step))) if step else (on(other, x, y),):
                 pl.semaphore_signal(barrier, inc=1, device_id=target, device_id_type=MESH)
-    pl.semaphore_signal(barrier, inc=1, device_id=on(source, x, y), device_id_type=MESH)
+
+    greet(before, range(SIDE))
+    greet(stage, range(1, SIDE))
+
+    @pl.when(stage == 0)
+    def _():
+        greet(after, range(SIDE))
+
     line = 2 * (SIDE - 1)
-    greeted = line + jnp.where(stage == stages - 1, 0, line + 1) + jnp.where(stage == 1, line + 1, 0)
+    greeted = 2 * line + 1 + jnp.where(stage == 1, line + 1, 0)
     pl.semaphore_wait(barrier, greeted)
 
     def remote(source, target, sent, received, device):
@@ -95,7 +102,7 @@
         wait_bytes(act_a.at[i], send_sem.at[2, i])
         wait_bytes(act_b.at[i], send_sem.at[3, i])
 
-    @pl.when(stage == 1)
+    @pl.when((stage == 1) | (stage == stages - 1))
     def _():
         for pair in range(pairs):
             rows = jnp.concatenate([tokens[2 * pair].astype(F32), tokens[2 * pair + 1].astype(F32)], axis=0).astype(BF16)
@@ -105,34 +112,45 @@
                 remote(tok_a.at[pair, y], tok_a.at[pair, y], tok_sem.at[0, pair], tok_sem.at[2, pair], on(stage, x, turn(y, step))).start()
                 remote(tok_b.at[pair, x], tok_b.at[pair, x], tok_sem.at[1, pair], tok_sem.at[3, pair], on(stage, turn(x, step), y)).start()
 
-        def bring(pair, carry):
+        def arrived(pair, carry):
             wait_bytes(tok_a.at[pair, pl.ds(0, SIDE - 1)], tok_sem.at[2, pair])
             wait_bytes(tok_b.at[pair, pl.ds(0, SIDE - 1)], tok_sem.at[3, pair])
-            for half_of_pair in range(2):
-                for parity in range(2):
-                    i = 4 * pair + 2 * half_of_pair + parity
-                    for p in range(pieces):
-                        at = slice(p * PIECE, (p + 1) * PIECE)
-                        own = slice(half_of_pair * OWN, (half_of_pair + 1) * OWN)
-                        for tok, out, mine in ((tok_a, out_a, x), (tok_b, out_b, y)):
-                            first = lax.rem(mine + parity, 2)
-                            out[i, p] = jnp.concatenate(
-                                [tok[pair, first + 2 * k, :, at].astype(F32)[own] for k in range(SIDE // 2)], axis=0
-                            ).astype(BF16)
-                        spread_a(i, p, stage - 1)
-                        spread_b(i, p, stage - 1)
-            return carry
-
-        lax.fori_loop(0, pairs, bring, 0)
+            return carry
+
+        def bring(i, carry):
+            pair, second, parity = i // 4, lax.rem(i // 2, 2), lax.rem(i, 2)
+            for p in range(pieces):
+                at = slice(p * PIECE, (p + 1) * PIECE)
+                for tok, out, mine in ((tok_a, out_a, x), (tok_b, out_b, y)):
+                    rows = [tok[pair, lax.rem(mine + parity, 2) + 2 * k, :, at].astype(F32) for k in range(SIDE // 2)]
+                    rows = [jnp.where(second == 0, value[:OWN], value[OWN:]) for value in rows]
+                    out[i, p] = jnp.concatenate(rows, axis=0).astype(BF16)
+                spread_a(i, p, 0)
+                spread_b(i, p, 0)
+            return carry
 
         def brought(pair, carry):
             wait_bytes(tok_a.at[pair, pl.ds(0, SIDE - 1)], tok_sem.at[0, pair])
             wait_bytes(tok_b.at[pair, pl.ds(0, SIDE - 1)], tok_sem.at[1, pair])
-            for k in range(4):
-                spread_sent(4 * pair + k)
-            return carry
+            return carry
+
+        def sent(i, carry):
+            spread_sent(i)
+            return carry
+
+        first = jnp.where(stage == 1, 0, NEAR)
+        last = jnp.where(stage == 1, NEAR, blocks)
+        arrived(0, 0)
+
+        @pl.when(stage == 1)
+        def _():
+            lax.fori_loop(0, min(4, NEAR), bring, 0)
+
+        lax.fori_loop(1, pairs, arrived, 0)
+        lax.fori_loop(jnp.where(stage == 1, min(4, NEAR), NEAR), last, bring, 0)
 
         lax.fori_loop(0, pairs, brought, 0)
+        lax.fori_loop(first, last, sent, 0)
 
     for load in loads:
         load.wait()

time: 305 us -> 290 us (0.951)
  Pallas kernels: 303 us -> 288 us
    pallas_call x1, Pallas kernels: 303 us -> 288 us  [local(): pl.pallas_call(functools.partial(kernel, stages, blocks), out_shape=jax.S...]
where the time goes in v4:
time: 290 us
  Pallas kernels  288 us (99%)
    pallas_call x1, Pallas kernels, local(): pl.pallas_call(functools.partial(kernel, stages, blocks), out_shape=jax.S...  288 us

profile of v4, /device:TPU:97, one launch (start us, length us, event | category | flops | bytes accessed | tf_op | source)
XLA Modules:
  0.0 290.2 jit_solution(17431251348387181265)
XLA Ops:
  0.0 288.3 %shard_map.55 = bf16[8,8,4096]{2,1,0:T(8,128)(2,1)} custom-call(bf16[8,8,4096]{2,1,0:T(8,128)(2,1)} %tokens.1, f32[1,4096]{1,0:T(1,128)} %gain.1, bf16[4096,896]{1,0:T(8,128)(2,1)} %bitcast.5, bf16[4096,896]{1,0:T(8,128)(2,1)} %bitcast.6, bf16[896,4096]{1,0:T(8,128)(2,1)} %bitcast.7), custom_call_target="tpu_custom_call" | custom-call | flops 22548578304 | bytes 22020096 | tf_op jit(solution)/shard_map/pallas_call | solution.py:338
  288.3 1.9 copy.7
